TPU v7x, 32 devices: a whole 2x2x4 slice. The times are simulated.
32 devices in a mesh: subj: 8 (over z, y), slab: 4 (over x, core).
Axes of the slice: x: 2, y: 2, z: 4, core: 2. Of those that a mesh axis runs over, the one named last changes fastest.
Arguments:
- image: float32 [8, 192, 8, 192], P('subj', 'slab'), may hold values from -6 to 6
- velocity: float32 [8, 3, 192, 8, 192], P('subj', None, 'slab'), may hold values from -3 to 3
- template: float32 [192, 8, 192], P('slab', 'subj'), may hold values from -6 to 6
- z_kernel: float32 [192, 192], replicated, as said below
- x_kernel: float32 [192, 192], replicated, as said below
Outputs:
- velocity_update: float32 [8, 3, 192, 8, 192], P('subj', None, 'slab')
- new_template: float32 [192, 8, 192], P('slab', 'subj')
Inputs may be any that keep to these rules, and one draw needn't show every extreme that they name: `z_kernel`: entries are positive. `x_kernel`: entries are positive.
All inputs are finite; a program needn't handle non-finite values.
Results may differ from a plain program's by a relative error of at most 0.00028.
Values sent between devices are 32-bit elements; how exact they have to be, the bound alone decides.
A program may use at most 64 MiB of HBM per device.

v0:
```python
import jax
import jax.numpy as jnp
from jax import lax
from jax.sharding import PartitionSpec as P


def with_halo(x, sides, width):
    for axis, dim in sides:
        size, length = (lax.axis_size(axis), x.shape[dim])
        up = [(i, (i + 1) % size) for i in range(size - 1)]
        down = [(j, i) for i, j in up]
        last = lax.slice_in_dim(x, length - width, length, axis=dim)
        leading = lax.slice_in_dim(x, 0, width, axis=dim)
        before = lax.ppermute(last, axis, up)
        after = lax.ppermute(leading, axis, down)
        x = jnp.concatenate([before, x, after], axis=dim)
    return x


def gradients(padded):
    slope_z = (padded[2:, 1:-1, 1:-1] - padded[:-2, 1:-1, 1:-1]) * 0.5
    slope_y = (padded[1:-1, 2:, 1:-1] - padded[1:-1, :-2, 1:-1]) * 0.5
    slope_x = (padded[1:-1, 1:-1, 2:] - padded[1:-1, 1:-1, :-2]) * 0.5
    return jnp.stack([slope_z, slope_y, slope_x])


def per_device(image, velocity, template, z_kernel, x_kernel):
    highest = lax.Precision.HIGHEST
    full_rows = lax.all_gather(template, "subj", axis=1, tiled=True)
    with_rims = with_halo(full_rows, (("slab", 0),), 1)
    padded = jnp.pad(with_rims, ((0, 0), (1, 1), (1, 1)))
    slopes = gradients(padded)
    warped = full_rows[None] + jnp.sum(velocity * slopes[None], 1)
    residual = image - warped
    forces = residual[:, None] * slopes[None]
    along_x = jnp.einsum("sczyx,wx->sczyw", forces, x_kernel, precision=highest)
    along_z = jnp.einsum(
        "vz,sczyx->scvyx",
        z_kernel,
        lax.all_to_all(along_x, "slab", split_axis=3, concat_axis=2, tiled=True),
        precision=highest,
    )
    velocity_update = lax.all_to_all(along_z, "slab", split_axis=2, concat_axis=3, tiled=True)
    local_sum = jnp.sum(residual, 0)
    subjects = lax.axis_size("subj") * image.shape[0]
    summed = lax.psum_scatter(local_sum, "subj", scatter_dimension=1, tiled=True)
    new_template = template + summed / subjects
    return (velocity_update, new_template)


def solution(mesh):
    in_specs = (
        P("subj", "slab", None, None),
        P("subj", None, "slab", None, None),
        P("slab", "subj", None),
        P(),
        P(),
    )
    out_specs = (P("subj", None, "slab", None, None), P("slab", "subj", None))
    return jax.shard_map(
        per_device, mesh=mesh, in_specs=in_specs, out_specs=out_specs, check_vma=False
    )
```

profile of v0, /device:TPU:0, one launch (start us, length us, event | category | flops | bytes accessed | tf_op | source)
XLA Modules:
  0.0 134.9 jit_solution(12613083913545052322)
XLA Ops:
  7.2 0.0 copy-start
  7.2 0.8 copy.29
  8.0 32.7 %all_gather.3 = f32[48,8,192]{2,0,1:T(8,128)S(1)} all-gather(f32[48,1,192]{2,0,1:T(8,128)S(1)} %copy.29), channel_id=1, replica_groups=mesh['subj'=8,'slab'=4] {'subj'}, dimensions={1}, use_global_device_ids=true | all-gather | bytes 331776 | tf_op jit(solution)/shard_map/all_gather | solution.py:29
  40.8 1.3 collective-permute-start.1
  42.1 1.3 collective-permute-start
  43.4 3.5 %collective-permute-done = f32[1,8,192]{2,0,1:T(1,128)S(1)} collective-permute-done((f32[1,8,192]{2,0,1:T(1,128)S(1)}, f32[1,8,192]{2,0,1:T(1,128)S(1)}, u32[]{:S(2)}, u32[]{:S(2)}) %collective-permute-start) | collective-permute-done | bytes 6176 | tf_op jit(solution)/shard_map/ppermute | solution.py:15
  46.9 0.2 select_maximum_fusion
  47.1 0.4 fusion.9
  47.5 0.8 copy-done.2
  48.4 0.5 fusion
  48.9 0.5 copy-done.3
  49.4 0.2 fusion.13
  49.5 0.1 fusion.2
  49.7 0.6 copy-done.1
  50.3 1.7 %convolution_bitcast_fusion.1 = f32[1,3,48,8,192]{4,3,2,1,0:T(8,128)S(1)} fusion(f32[3,48,8,192]{3,1,2,0:T(8,128)S(1)} %fusion.2, f32[192,192]{1,0:T(8,128)S(1)} %copy-done), kind=kOutput, calls=%fused_computation.1 | convolution fusion | flops 509607936 | bytes 1916928 | tf_op jit(solution)/shard_map/sczyx,wx->sczyw/dot_general | solution.py:36
  52.0 1.4 %copy.33 = f32[1,3,48,8,192]{4,2,1,0,3:T(8,128)} copy(f32[1,3,48,8,192]{4,3,2,1,0:T(8,128)S(1)} %convolution_bitcast_fusion.1) | data formatting | bytes 1769472 | tf_op jit(solution)/shard_map/sczyx,wx->sczyw/dot_general | solution.py:36
  53.3 3.7 %all-to-all-start = ((f32[1,3,48,8,192]{4,2,1,0,3:T(8,128)}), f32[1,3,48,8,192]{4,2,1,0,3:T(8,128)S(1)}, u32[]{:S(2)}, u32[]{:S(2)}) async-start(f32[1,3,48,8,192]{4,2,1,0,3:T(8,128)} %copy.33), calls=%async_computation | async-start | bytes 2359296 | tf_op jit(solution)/shard_map/all_to_all | solution.py:40
  57.0 0.7 reduce-scatter.2.cloned.1.call-update
  57.7 15.1 %all-to-all-done = f32[1,3,48,8,192]{4,2,1,0,3:T(8,128)S(1)} async-done(((f32[1,3,48,8,192]{4,2,1,0,3:T(8,128)}), f32[1,3,48,8,192]{4,2,1,0,3:T(8,128)S(1)}, u32[]{:S(2)}, u32[]{:S(2)}) %all-to-all-start) | async-done | bytes 884768 | tf_op jit(solution)/shard_map/all_to_all | solution.py:40
  72.9 0.1 copy.34
  73.0 0.0 copy-start.4
  73.0 0.1 copy.35
  73.1 0.8 copy-done.4
  73.9 2.3 %convolution_bitcast_fusion = f32[1,3,192,2,192]{2,4,3,1,0:T(8,128)S(1)} fusion(f32[3,192,2,192]{3,1,2,0:T(8,128)S(1)} %bitcast.41, f32[192,192]{1,0:T(8,128)S(1)} %copy-done.4), kind=kOutput, calls=%fused_computation | convolution fusion | flops 509607936 | bytes 1916928 | tf_op jit(solution)/shard_map/vz,sczyx->scvyx/dot_general | solution.py:37
  76.3 1.5 %copy.37 = f32[1,3,192,2,192]{4,3,1,0,2:T(2,128)} copy(f32[1,3,192,2,192]{2,4,3,1,0:T(8,128)S(1)} %convolution_bitcast_fusion) | data formatting | bytes 1769472 | tf_op jit(solution)/shard_map/vz,sczyx->scvyx/transpose | solution.py:37
  77.8 3.7 %all-to-all-start.1 = ((f32[1,3,192,2,192]{4,3,1,0,2:T(2,128)}), f32[1,3,192,2,192]{4,3,1,0,2:T(2,128)S(1)}, u32[]{:S(2)}, u32[]{:S(2)}) async-start(f32[1,3,192,2,192]{4,3,1,0,2:T(2,128)} %copy.37), calls=%async_computation.1 | async-start | bytes 2359296 | tf_op jit(solution)/shard_map/all_to_all | solution.py:43
  81.4 43.2 %reduce-scatter.2.cloned.1.call-done = f32[48,1,192]{2,0,1:T(8,128)} async-done(((f32[48,8,192]{2,0,1:T(8,128)}), f32[48,1,192]{2,0,1:T(8,128)}) %reduce-scatter.2.cloned.1.call-update) | async-done | bytes 36880 | tf_op jit(solution)/shard_map/reduce_scatter | solution.py:46
  124.6 0.8 multiply_add_fusion
  125.4 0.7 copy.42
  126.1 0.1 copy.38
  126.2 0.1 copy.39
  126.3 1.7 %copy.41 = f32[1,3,48,8,192]{4,3,2,1,0:T(8,128)} copy(f32[1,3,48,8,192]{4,2,3,1,0:T(8,128)S(1)} %bitcast.44) | data formatting | bytes 1769472
  (10 shorter events, 0.0 us)
Async XLA Ops:
  7.2 43.1 %copy-start = (f32[192,192]{1,0:T(8,128)S(1)}, f32[192,192]{1,0:T(8,128)}, u32[]{:S(2)}) copy-start(f32[192,192]{1,0:T(8,128)} %param.9) | copy-start | bytes 442372
  40.8 2.6 %collective-permute-start.1 = (f32[1,8,192]{2,0,1:T(1,128)S(1)}, f32[1,8,192]{2,0,1:T(1,128)S(1)}, u32[]{:S(2)}, u32[]{:S(2)}) collective-permute-start(f32[1,8,192]{2,0,1:T(1,128)S(1)} %get-tuple-element.10), channel_id=1, source_target_pairs={{0,1},{1,2},{2,3},{4,5},{5,6},{6,7},{8,9},{9,10},{10,11},{12,13},{... | collective-permute-start | bytes 18440 | tf_op jit(solution)/shard_map/ppermute | solution.py:14
  42.1 4.8 %collective-permute-start = (f32[1,8,192]{2,0,1:T(1,128)S(1)}, f32[1,8,192]{2,0,1:T(1,128)S(1)}, u32[]{:S(2)}, u32[]{:S(2)}) collective-permute-start(f32[1,8,192]{2,0,1:T(1,128)S(1)} %get-tuple-element.11), channel_id=1, source_target_pairs={{1,0},{2,1},{3,2},{5,4},{6,5},{7,6},{9,8},{10,9},{11,10},{13,12},{... | collective-permute-start | bytes 18440 | tf_op jit(solution)/shard_map/ppermute | solution.py:15
  47.1 1.3 copy-start.2
  48.4 1.0 copy-start.3
  49.5 0.7 copy-start.1
  53.3 19.5 %all-to-all-start = ((f32[1,3,48,8,192]{4,2,1,0,3:T(8,128)}), f32[1,3,48,8,192]{4,2,1,0,3:T(8,128)S(1)}, u32[]{:S(2)}, u32[]{:S(2)}) async-start(f32[1,3,48,8,192]{4,2,1,0,3:T(8,128)} %copy.33), calls=%async_computation | async-start | bytes 2359296 | tf_op jit(solution)/shard_map/all_to_all | solution.py:40
  57.0 67.6 %reduce-scatter.2.cloned.1.call-start = ((), (), s32[]{:S(2)}) async-start(), calls=%async_computation.3 | async-start | bytes 442368 | tf_op jit(solution)/shard_map/reduce_scatter | solution.py:46
  73.0 0.9 copy-start.4
  77.8 46.9 %copy-start.5 = (f32[48,1,192]{2,1,0:T(1,128)S(1)}, f32[48,1,192]{2,1,0:T(1,128)}, u32[]{:S(2)}) copy-start(f32[48,1,192]{2,1,0:T(1,128)} %param.7) | copy-start | bytes 110596
  77.8 48.3 %all-to-all-start.1 = ((f32[1,3,192,2,192]{4,3,1,0,2:T(2,128)}), f32[1,3,192,2,192]{4,3,1,0,2:T(2,128)S(1)}, u32[]{:S(2)}, u32[]{:S(2)}) async-start(f32[1,3,192,2,192]{4,3,1,0,2:T(2,128)} %copy.37), calls=%async_computation.1 | async-start | bytes 2359296 | tf_op jit(solution)/shard_map/all_to_all | solution.py:43
Sparse Core Ops, SparseCore 0:
  61.1 63.4 reduce-scatter.1
where the time goes:
time: 135 us
  waiting for transfers between devices  62.5 us (46%)
  blocking collectives  32.7 us (24%)
  between operations  14.2 us (11%)
  starting transfers between devices  9.92 us (7%)
  local copies, waits for them, and re-layouts  9.25 us (7%)
  matrix products  4.01 us (3%)
  other arithmetic  2.26 us (2%)
    reduce_scatter x1, waiting for transfers between devices, per_device(): lax.psum_scatter(local_sum, 'subj', scatter_dimension=1, tiled=True)  43.2 us
    all_gather x1, blocking collectives, per_device(): full_rows = lax.all_gather(template, 'subj', axis=1, tiled=True)  32.7 us
    all_to_all x1, waiting for transfers between devices, per_device(): lax.all_to_all(along_x, 'slab', split_axis=3, concat_axis=2, tiled=True)  15.1 us
    unnamed x15, local copies, waits for them, and re-layouts  5.96 us
    all_to_all x1, starting transfers between devices, per_device(): lax.all_to_all(along_x, 'slab', split_axis=3, concat_axis=2, tiled=True)  3.67 us
    all_to_all x1, starting transfers between devices, per_device(): lax.all_to_all(along_z, 'slab', split_axis=2, concat_axis=3, tiled=True)  3.66 us
    ppermute x1, waiting for transfers between devices, with_halo(): after = lax.ppermute(leading, axis, down)  3.48 us
  transfers between devices with their start and end apart: 5, of which 3 were waited for; matrix products, arithmetic and copies ran while one was open for 4% of the time, Pallas kernels for 0%

commit v1 on v0

v1 whole, which is shorter than its diff:
```python
import functools

import jax
import jax.numpy as jnp
from jax import lax
from jax.experimental import pallas as pl
from jax.experimental.pallas import tpu as pltpu
from jax.sharding import PartitionSpec as P

MESH = pl.DeviceIdType.MESH


def split(x):
    hi = x.astype(jnp.bfloat16)
    return hi, (x - hi.astype(jnp.float32)).astype(jnp.bfloat16)


def dot(a, b):
    return jnp.dot(a, b, preferred_element_type=jnp.float32)


def x_slope(t):
    zero = jnp.zeros((t.shape[0], 1), t.dtype)
    after = jnp.concatenate([t[:, 1:], zero], axis=1)
    before = jnp.concatenate([zero, t[:, :-1]], axis=1)
    return (after - before) * 0.5


def z_slope(t, low, high):
    after = jnp.concatenate([t[1:], high], axis=0)
    before = jnp.concatenate([low, t[:-1]], axis=0)
    return (after - before) * 0.5


def kernel(
    n_subj, n_slab, dz, nx,
    image, velocity, template, zk, xk, out, new_t,
    img_v, vel_v, row_v, zk_v, xk_v, T, R, E, acc, zs, xs, o_v, nt_v,
    loc, t_recv, r_recv, e_recv, a_recv,
    s1, s2, s3, s4, r3, r4, es, as_,
):
    ny = n_subj
    nz = n_slab * dz
    mirrors = n_slab // 2
    outer = n_subj // 2
    s = lax.axis_index("subj")
    k = lax.axis_index("slab")
    par, so = s % 2, s // 2
    core, km = k % 2, k // 2
    partner = so * 2 + 1 - par
    sib = km * 2 + 1 - core

    cps = [
        pltpu.make_async_copy(template, row_v, loc.at[0]),
        pltpu.make_async_copy(image, img_v, loc.at[1]),
        pltpu.make_async_copy(velocity, vel_v, loc.at[2]),
        pltpu.make_async_copy(zk, zk_v, loc.at[3]),
        pltpu.make_async_copy(xk, xk_v, loc.at[4]),
    ]
    for c in cps:
        c.start()

    E[...] = jnp.zeros_like(E)
    T[0] = jnp.zeros_like(T[0])
    T[ny + 1] = jnp.zeros_like(T[ny + 1])

    barrier = pltpu.get_barrier_semaphore()

    def hello(ds, dk):
        pl.semaphore_signal(barrier, inc=1, device_id={"subj": ds, "slab": dk}, device_id_type=MESH)

    for i in range(1, n_subj):
        hello((s + i) % n_subj, k)
    for i in range(n_subj):
        @pl.when(k > 0)
        def _():
            hello((s + i) % n_subj, k - 1)

        @pl.when(k < n_slab - 1)
        def _():
            hello((s + i) % n_subj, k + 1)
    for j in range(n_slab):
        @pl.when((j != k) & (j != k - 1) & (j != k + 1) & ((j % 2 == core) | (j == sib)))
        def _():
            hello(s, j)

    def rdma(src, dst, ss, rs, ds, dk):
        return pltpu.make_async_remote_copy(
            src_ref=src, dst_ref=dst, send_sem=ss, recv_sem=rs,
            device_id={"subj": ds, "slab": dk}, device_id_type=MESH,
        )

    def edge_up(i):
        d = (s + i) % n_subj
        return rdma(row_v.at[dz - 1], E.at[0, s], es.at[0, i], e_recv.at[0, s], d, k + 1)

    def edge_down(i):
        d = (s + i) % n_subj
        return rdma(row_v.at[0], E.at[1, s], es.at[1, i], e_recv.at[1, s], d, k - 1)

    def send1(i):
        d = ((so + i) % outer) * 2 + par
        return rdma(T.at[s + 1, k], T.at[s + 1, k], s1.at[i], t_recv.at[s, k], d, k)

    def send2(y):
        return rdma(T.at[y + 1, k], T.at[y + 1, k], s2.at[y // 2], t_recv.at[y, k], partner, k)

    def send3(y, m):
        dk = ((km + m) % mirrors) * 2 + core
        return rdma(T.at[y + 1, k], T.at[y + 1, k], s3.at[y, m], t_recv.at[y, k], s, dk)

    def send4(y, m):
        kk = ((km + m) % mirrors) * 2 + core
        return rdma(T.at[y + 1, kk], T.at[y + 1, kk], s4.at[y, m], t_recv.at[y, kk], s, sib)

    def got_t(y, kk):
        rdma(T.at[y + 1, kk], T.at[y + 1, kk], s4.at[0, 0], t_recv.at[y, kk], s, sib).wait_recv()

    def rsend3(y, m):
        dk = ((km + m) % mirrors) * 2 + core
        return rdma(R.at[y, k], R.at[y, k], r3.at[y, m], r_recv.at[y, k], s, dk)

    def rsend4(y, m):
        kk = ((km + m) % mirrors) * 2 + core
        return rdma(R.at[y, kk], R.at[y, kk], r4.at[y, m], r_recv.at[y, kk], s, sib)

    def got_r(y, kk):
        rdma(R.at[y, kk], R.at[y, kk], r4.at[0, 0], r_recv.at[y, kk], s, sib).wait_recv()

    def asend(y):
        return rdma(R.at[y, k], acc.at[s], as_.at[y], a_recv.at[s], y, k)

    cps[0].wait()
    T[s + 1, k] = row_v[:, 0, :]

    n_hello = n_subj - 1
    for j in range(n_slab):
        @pl.when(j == k)
        def _():
            near = [i for i in (j - 1, j + 1) if 0 <= i < n_slab]
            far = [i for i in range(n_slab) if i != j and i not in near and (i % 2 == j % 2 or i == (j ^ 1))]
            pl.semaphore_wait(barrier, n_hello + n_subj * len(near) + len(far))

    for i in range(1, outer):
        send1(i).start()
    send2(s).start()
    for i in range(n_subj):
        @pl.when(k < n_slab - 1)
        def _():
            edge_up(i).start()

        @pl.when(k > 0)
        def _():
            edge_down(i).start()

    def spread(y):
        for m in range(1, mirrors):
            send3(y, m).start()
        send4(y, 0).start()

    spread(s)
    for i in range(1, outer):
        y = ((so + i) % outer) * 2 + par
        got_t(y, k)
        send2(y).start()
        spread(y)
    for i in range(outer):
        y = ((so + i) % outer) * 2 + 1 - par
        got_t(y, k)
        spread(y)

    def wait_edge(side):
        def body(y, _):
            rdma(row_v.at[0], E.at[side, y], es.at[0, 0], e_recv.at[side, y], s, k).wait_recv()
            return 0
        lax.fori_loop(0, ny, body, 0)

    @pl.when(k > 0)
    def _():
        wait_edge(0)

    @pl.when(k < n_slab - 1)
    def _():
        wait_edge(1)

    cps[1].wait()
    cps[2].wait()

    def residual(y, _):
        t = T[y + 1, k]
        sz = z_slope(t, E[0, y], E[1, y])
        sy = (T[y + 2, k] - T[y, k]) * 0.5
        sx = x_slope(t)
        rows = pl.ds(y, dz, stride=ny)

        def pick(ref):
            return jnp.concatenate([h[rows, :] for h in ref], axis=1)

        v = [vel_v[c, :, y, :] for c in range(3)]
        r = img_v[:, y, :] - (t + (v[0] * sz + v[1] * sy + v[2] * sx))
        R[y, k] = r
        for m in range(1, mirrors):
            rsend3(y, m).start()
        rsend4(y, 0).start()

        @pl.when(y != s)
        def _():
            asend(y).start()
        return 0

    lax.fori_loop(0, ny, residual, 0)

    cps[3].wait()
    cps[4].wait()
    for j in range(n_slab):
        @pl.when(j == k)
        def _():
            hi, lo = split(zk_v[j * dz:(j + 1) * dz, :])
            zs[0] = hi
            zs[1] = lo
    hi, lo = split(xk_v[...].T)
    xs[0] = hi
    xs[1] = lo

    def mirror_t(y, _):
        for m in range(1, mirrors):
            got_t(y, ((km + m) % mirrors) * 2 + core)
            send4(y, m).start()
        return 0

    lax.fori_loop(0, ny, mirror_t, 0)

    def sibling_t(y, _):
        for m in range(mirrors):
            got_t(y, m * 2 + 1 - core)
        return 0

    lax.fori_loop(0, ny, sibling_t, 0)

    def mirror_r(y):
        for m in range(1, mirrors):
            got_r(y, ((km + m) % mirrors) * 2 + core)
            rsend4(y, m).start()

    def smooth(y):
        for m in range(mirrors):
            got_r(y, m * 2 + 1 - core)
        whole = (nz, nx)
        t = T[y + 1].reshape(whole)
        zero = jnp.zeros((1, nx), jnp.float32)
        r = R[y].reshape(whole)
        slopes = (
            z_slope(t, zero, zero),
            (T[y + 2].reshape(whole) - T[y].reshape(whole)) * 0.5,
            x_slope(t),
        )
        zh, zl = zs[0], zs[1]
        xh, xl = xs[0], xs[1]
        for c in range(3):
            fh, fl = split(r * slopes[c])
            a = dot(zh, fh) + (dot(zh, fl) + dot(zl, fh))
            ah, al = split(a)
            o_v[c, :, y, :] = dot(ah, xh) + (dot(ah, xl) + dot(al, xh))

    mirror_r(0)

    def steps(y, _):
        @pl.when(y + 1 < ny)
        def _():
            mirror_r(y + 1)
        smooth(y)
        return 0

    lax.fori_loop(0, ny, steps, 0)
    o_cp = pltpu.make_async_copy(o_v, out, loc.at[5])
    o_cp.start()

    total = R[s, k]
    for i in range(1, n_subj):
        j = (s + i) % n_subj
        rdma(R.at[0, 0], acc.at[j], as_.at[0], a_recv.at[j], s, k).wait_recv()
        total = total + acc[j]
    nt_v[:, 0, :] = T[s + 1, k] + total / n_subj
    n_cp = pltpu.make_async_copy(nt_v, new_t, loc.at[6])
    n_cp.start()

    for i in range(1, outer):
        send1(i).wait_send()
    for i in range(outer):
        send2(((so + i) % outer) * 2 + par).wait_send()

    def drain(y, _):
        for m in range(1, mirrors):
            send3(y, m).wait_send()
            rsend3(y, m).wait_send()
        for m in range(mirrors):
            send4(y, m).wait_send()
            rsend4(y, m).wait_send()

        @pl.when(y != s)
        def _():
            asend(y).wait_send()

        @pl.when(k < n_slab - 1)
        def _():
            edge_up(y).wait_send()

        @pl.when(k > 0)
        def _():
            edge_down(y).wait_send()
        return 0

    lax.fori_loop(0, ny, drain, 0)
    o_cp.wait()
    n_cp.wait()


def per_device(image, velocity, template, z_kernel, x_kernel):
    n_subj, n_slab = lax.axis_size("subj"), lax.axis_size("slab")
    _, dz, ny, nx = image.shape
    nz = n_slab * dz
    mirrors, outer = n_slab // 2, n_subj // 2
    f32, bf16 = jnp.float32, jnp.bfloat16
    dma = pltpu.SemaphoreType.DMA
    any_ = pl.BlockSpec(memory_space=pl.ANY)
    update, new_template = pl.pallas_call(
        functools.partial(kernel, n_subj, n_slab, dz, nx),
        out_shape=(
            jax.ShapeDtypeStruct((3, dz, ny, nx), f32),
            jax.ShapeDtypeStruct(template.shape, f32),
        ),
        in_specs=[any_] * 5,
        out_specs=(any_, any_),
        scratch_shapes=[
            pltpu.VMEM((dz, ny, nx), f32),
            pltpu.VMEM((3, dz, ny, nx), f32),
            pltpu.VMEM((dz, 1, nx), f32),
            pltpu.VMEM((nz, nz), f32),
            pltpu.VMEM((nx, nx), f32),
            pltpu.VMEM((ny + 2, n_slab, dz, nx), f32),
            pltpu.VMEM((ny, n_slab, dz, nx), f32),
            pltpu.VMEM((2, ny, 1, nx), f32),
            pltpu.VMEM((ny, dz, nx), f32),
            pltpu.VMEM((2, dz, nz), bf16),
            pltpu.VMEM((2, nx, nx), bf16),
            pltpu.VMEM((3, dz, ny, nx), f32),
            pltpu.VMEM((dz, 1, nx), f32),
            dma((7,)),
            dma((ny, n_slab)),
            dma((ny, n_slab)),
            dma((2, ny)),
            dma((ny,)),
            dma((outer,)),
            dma((outer,)),
            dma((ny, mirrors)),
            dma((ny, mirrors)),
            dma((ny, mirrors)),
            dma((ny, mirrors)),
            dma((2, ny)),
            dma((ny,)),
        ],
        compiler_params=pltpu.CompilerParams(
            collective_id=0, has_side_effects=True, vmem_limit_bytes=56 * 1024 * 1024
        ),
    )(image[0], velocity[0], template, z_kernel, x_kernel)
    return update[None], new_template


def solution(mesh):
    in_specs = (
        P("subj", "slab", None, None),
        P("subj", None, "slab", None, None),
        P("slab", "subj", None),
        P(),
        P(),
    )
    out_specs = (P("subj", None, "slab", None, None), P("slab", "subj", None))
    return jax.shard_map(
        per_device, mesh=mesh, in_specs=in_specs, out_specs=out_specs, check_vma=False
    )
```

time: 135 us -> 36.6 us (0.27)
  waiting for transfers between devices: 62.5 us -> 0 us
  Pallas kernels: 0 us -> 32.8 us
  blocking collectives: 32.7 us -> 0 us
  between operations: 14.2 us -> 0.65 us
  starting transfers between devices: 9.92 us -> 0 us
  local copies, waits for them, and re-layouts: 9.25 us -> 3 us
  matrix products: 4.01 us -> 0 us
  other arithmetic: 2.26 us -> 0 us
    reduce_scatter x1 -> x0, waiting for transfers between devices: 43.2 us -> none  [per_device(): lax.psum_scatter(local_sum, 'subj', scatter_dimension=1, tiled=True)]
    pallas_call x0 -> x1, Pallas kernels: none -> 32.8 us  [per_device(): pl.pallas_call(functools.partial(kernel, n_subj, n_slab, dz, nx), out_sha...]
    all_gather x1 -> x0, blocking collectives: 32.7 us -> none  [per_device(): full_rows = lax.all_gather(template, 'subj', axis=1, tiled=True)]
    all_to_all x2 -> x0, waiting for transfers between devices: 15.2 us -> none  [the longest x1 15.1 us: per_device(): lax.all_to_all(along_x, 'slab', split_axis=3, concat_axis=2, tiled=True)]
    all_to_all x2 -> x0, starting transfers between devices: 7.33 us -> none  [the longest x1 3.67 us: per_device(): lax.all_to_all(along_x, 'slab', split_axis=3, concat_axis=2, tiled=True)]
    dot_general x2 -> x0, matrix products: 4.01 us -> none  [the longest x1 2.33 us: per_device(): jnp.einsum('vz,sczyx->scvyx', z_kernel, lax.all_to_all(along_x, 'slab', s...]
    ppermute x2 -> x0, waiting for transfers between devices: 3.49 us -> none  [the longest x1 3.48 us: with_halo(): after = lax.ppermute(leading, axis, down)]
    unnamed x15 -> x4, local copies, waits for them, and re-layouts: 5.96 us -> 3 us
  transfers between devices with their start and end apart: 5 -> 0, of which waited for: 3 -> 0; matrix products, arithmetic and copies ran while one was open for 4% -> 0% of each run, Pallas kernels for 0% -> 0%
where the time goes in v1:
time: 36.6 us; the launch traced here: 36.5 us
  Pallas kernels  32.8 us (90%)
  local copies, waits for them, and re-layouts  3 us (8%)
  between operations  0.65 us (2%)
    pallas_call x1, Pallas kernels, per_device(): pl.pallas_call(functools.partial(kernel, n_subj, n_slab, dz, nx), out_sha...  32.8 us
    unnamed x4, local copies, waits for them, and re-layouts  3 us

profile of v1, /device:TPU:0, one launch (start us, length us, event | category | flops | bytes accessed | tf_op | source)
XLA Modules:
  0.0 36.5 jit_solution(8887920879609329643)
XLA Ops:
  0.6 32.8 %shard_map.68 = (f32[3,48,8,192]{3,2,1,0:T(8,128)}, f32[48,1,192]{2,1,0:T(1,128)}) custom-call(f32[48,8,192]{2,1,0:T(8,128)} %bitcast.5, f32[3,48,8,192]{3,2,1,0:T(8,128)} %bitcast.4, f32[48,1,192]{2,1,0:T(1,128)} %template.1, f32[192,192]{1,0:T(8,128)} %zk.1, f32[192,192]{1,0:T(8,128)} %xk.1), custom_call_target="tpu_custom_call" | custom-call | tf_op jit(solution)/shard_map/pallas_call | solution.py:326
  33.5 0.0 copy-start
  33.5 2.4 %copy.9 = f32[1,3,48,8,192]{4,3,2,1,0:T(8,128)} copy(f32[1,3,48,8,192]{4,3,2,1,0:T(8,128)} %bitcast.3) | data formatting | bytes 1769472
  35.8 0.0 copy-done
  35.8 0.6 %copy.10 = f32[48,1,192]{2,1,0:T(1,128)} copy(f32[48,1,192]{2,1,0:T(1,128)S(1)} %copy-done) | data formatting | bytes 73728
Async XLA Ops:
  33.5 2.4 %copy-start = (f32[48,1,192]{2,1,0:T(1,128)S(1)}, f32[48,1,192]{2,1,0:T(1,128)}, u32[]{:S(2)}) copy-start(f32[48,1,192]{2,1,0:T(1,128)} %get-tuple-element.9) | copy-start | bytes 110596

commit v2 on v1

v2 whole, which is shorter than its diff:
```python
import functools

import jax
import jax.numpy as jnp
from jax import lax
from jax.experimental import pallas as pl
from jax.experimental.pallas import tpu as pltpu
from jax.sharding import PartitionSpec as P

MESH = pl.DeviceIdType.MESH


def split(x):
    hi = x.astype(jnp.bfloat16)
    return hi, (x - hi.astype(jnp.float32)).astype(jnp.bfloat16)


def dot(a, b):
    return jnp.dot(a, b, preferred_element_type=jnp.float32)


def pack(x):
    dz, nx = x.shape
    rem = nx % 128
    fold = 128 // rem
    step = dz // fold
    tail = x[:, nx - rem:]
    parts = [tail[i * step:(i + 1) * step] for i in range(fold)]
    return jnp.concatenate([x[:, :128], jnp.concatenate(parts, axis=1)], axis=0)


def unpack(x, dz, nx):
    rem = nx % 128
    fold = 128 // rem
    tail = x[..., dz:, :]
    parts = [tail[..., i * rem:(i + 1) * rem] for i in range(fold)]
    tail = jnp.concatenate(parts, axis=-2)
    x = jnp.concatenate([x[..., :dz, :], tail], axis=-1)
    return x.reshape(-1, nx)


def x_slope(t):
    zero = jnp.zeros((t.shape[0], 1), t.dtype)
    after = jnp.concatenate([t[:, 1:], zero], axis=1)
    before = jnp.concatenate([zero, t[:, :-1]], axis=1)
    return (after - before) * 0.5


def z_slope(t, low, high):
    after = jnp.concatenate([t[1:], high], axis=0)
    before = jnp.concatenate([low, t[:-1]], axis=0)
    return (after - before) * 0.5


def kernel(
    n_subj, n_slab, dz, nx,
    image, velocity, template, zk, xk, o_v, nt_v,
    img_v, vel_v, row_v, zk_v, xk_v, T, R, S, E, acc, zs, xs,
    loc, in_sem, t_recv, r_recv, e_recv, a_recv,
    s1, s2, s3, s4, r3, r4, es, as_,
):
    ny = n_subj
    nz = n_slab * dz
    mirrors = n_slab // 2
    outer = n_subj // 2
    s = lax.axis_index("subj")
    k = lax.axis_index("slab")
    par, so = s % 2, s // 2
    core, km = k % 2, k // 2
    partner = so * 2 + 1 - par
    sib = km * 2 + 1 - core

    cps = [
        pltpu.make_async_copy(template, row_v, loc.at[0]),
        pltpu.make_async_copy(zk, zk_v, loc.at[1]),
        pltpu.make_async_copy(xk, xk_v, loc.at[2]),
    ]
    for c in cps:
        c.start()

    def row_in(y):
        return [pltpu.make_async_copy(image.at[:, y, :], img_v.at[y], in_sem.at[3, y])] + [
            pltpu.make_async_copy(velocity.at[c, :, y, :], vel_v.at[c, y], in_sem.at[c, y])
            for c in range(3)
        ]

    def load_rows(y, _):
        for c in row_in(y):
            c.start()
        return 0

    E[...] = jnp.zeros_like(E)
    T[0] = jnp.zeros_like(T[0])
    T[ny + 1] = jnp.zeros_like(T[ny + 1])

    barrier = pltpu.get_barrier_semaphore()

    def hello(ds, dk):
        pl.semaphore_signal(barrier, inc=1, device_id={"subj": ds, "slab": dk}, device_id_type=MESH)

    for i in range(1, n_subj):
        hello((s + i) % n_subj, k)
    for i in range(n_subj):
        @pl.when(k > 0)
        def _():
            hello((s + i) % n_subj, k - 1)

        @pl.when(k < n_slab - 1)
        def _():
            hello((s + i) % n_subj, k + 1)
    for j in range(n_slab):
        @pl.when((j != k) & (j != k - 1) & (j != k + 1) & ((j % 2 == core) | (j == sib)))
        def _():
            hello(s, j)

    def rdma(src, dst, ss, rs, ds, dk):
        return pltpu.make_async_remote_copy(
            src_ref=src, dst_ref=dst, send_sem=ss, recv_sem=rs,
            device_id={"subj": ds, "slab": dk}, device_id_type=MESH,
        )

    def edge_up(i):
        d = (s + i) % n_subj
        return rdma(row_v.at[dz - 1], E.at[0, s], es.at[0, i], e_recv.at[0, s], d, k + 1)

    def edge_down(i):
        d = (s + i) % n_subj
        return rdma(row_v.at[0], E.at[1, s], es.at[1, i], e_recv.at[1, s], d, k - 1)

    def send1(i):
        d = ((so + i) % outer) * 2 + par
        return rdma(T.at[s + 1, k], T.at[s + 1, k], s1.at[i], t_recv.at[s, k], d, k)

    def slab_of(m):
        return ((km + m) % mirrors) * 2 + core

    def send2(y, m):
        kk = slab_of(m)
        return rdma(T.at[y + 1, kk], T.at[y + 1, kk], s2.at[y // 2, m], t_recv.at[y, kk], partner, k)

    def send3(y, m):
        dk = slab_of(m)
        return rdma(T.at[y + 1, k], T.at[y + 1, k], s3.at[y // 2, m], t_recv.at[y, k], s, dk)

    def send4(y, m):
        kk = slab_of(m)
        return rdma(T.at[y + 1, kk], T.at[y + 1, kk], s4.at[y, m], t_recv.at[y, kk], s, sib)

    def got_t(y, kk):
        rdma(T.at[y + 1, kk], T.at[y + 1, kk], s4.at[0, 0], t_recv.at[y, kk], s, sib).wait_recv()

    def rsend3(y, m):
        dk = slab_of(m)
        return rdma(R.at[y, k], R.at[y, k], r3.at[y, m], r_recv.at[y, k], s, dk)

    def rsend4(y, m):
        kk = slab_of(m)
        return rdma(R.at[y, kk], R.at[y, kk], r4.at[y, m], r_recv.at[y, kk], s, sib)

    def got_r(y, kk):
        rdma(R.at[y, kk], R.at[y, kk], r4.at[0, 0], r_recv.at[y, kk], s, sib).wait_recv()

    def asend(y):
        return rdma(R.at[y, k], acc.at[s], as_.at[y], a_recv.at[s], y, k)

    cps[0].wait()
    T[s + 1, k] = pack(row_v[:, 0, :])

    n_hello = n_subj - 1
    for j in range(n_slab):
        @pl.when(j == k)
        def _():
            near = [i for i in (j - 1, j + 1) if 0 <= i < n_slab]
            far = [i for i in range(n_slab) if i != j and i not in near and (i % 2 == j % 2 or i == (j ^ 1))]
            pl.semaphore_wait(barrier, n_hello + n_subj * len(near) + len(far))

    for i in range(1, outer):
        send1(i).start()
    send2(s, 0).start()
    for i in range(n_subj):
        @pl.when(k < n_slab - 1)
        def _():
            edge_up(i).start()

        @pl.when(k > 0)
        def _():
            edge_down(i).start()

    for m in range(1, mirrors):
        send3(s, m).start()
    lax.fori_loop(0, ny, load_rows, 0)
    send4(s, 0).start()
    for i in range(1, outer):
        y = ((so + i) % outer) * 2 + par
        got_t(y, k)
        send2(y, 0).start()
        for m in range(1, mirrors):
            send3(y, m).start()
        send4(y, 0).start()
    for i in range(outer):
        y = ((so + i) % outer) * 2 + 1 - par
        got_t(y, k)
        send4(y, 0).start()

    def wait_edge(side):
        def body(y, _):
            rdma(row_v.at[0], E.at[side, y], es.at[0, 0], e_recv.at[side, y], s, k).wait_recv()
            return 0
        lax.fori_loop(0, ny, body, 0)

    @pl.when(k > 0)
    def _():
        wait_edge(0)

    @pl.when(k < n_slab - 1)
    def _():
        wait_edge(1)

    def residual(y, _):
        t = unpack(T[y + 1, k], dz, nx)
        sz = z_slope(t, E[0, y], E[1, y])
        sy = unpack((T[y + 2, k] - T[y, k]) * 0.5, dz, nx)
        sx = x_slope(t)
        for c in row_in(y):
            c.wait()
        v = [vel_v[c, y] for c in range(3)]
        R[y, k] = pack(img_v[y] - (t + (v[0] * sz + v[1] * sy + v[2] * sx)))
        for m in range(1, mirrors):
            rsend3(y, m).start()
        rsend4(y, 0).start()

        @pl.when(y != s)
        def _():
            asend(y).start()

        @pl.when(y < outer)
        def _():
            yy = ((so + y) % outer) * 2 + par
            for m in range(1, mirrors):
                got_t(yy, slab_of(m))
                send2(yy, m).start()
                send4(yy, m).start()
        return 0

    lax.fori_loop(0, ny, residual, 0)

    cps[1].wait()
    cps[2].wait()
    for j in range(n_slab):
        @pl.when(j == k)
        def _():
            hi, lo = split(zk_v[j * dz:(j + 1) * dz, :])
            zs[0] = hi
            zs[1] = lo
    hi, lo = split(xk_v[...].T)
    xs[0] = hi
    xs[1] = lo

    for i in range(outer):
        y = ((so + i) % outer) * 2 + 1 - par
        for m in range(1, mirrors):
            got_t(y, slab_of(m))
            send4(y, m).start()

    def sibling_t(y, _):
        for m in range(mirrors):
            got_t(y, m * 2 + 1 - core)
        return 0

    lax.fori_loop(0, ny, sibling_t, 0)

    def slopes(y, _):
        zero = jnp.zeros((1, nx), jnp.float32)
        t = unpack(T[y + 1], dz, nx)
        S[y, 0] = z_slope(t, zero, zero)
        S[y, 1] = unpack((T[y + 2] - T[y]) * 0.5, dz, nx)
        S[y, 2] = x_slope(t)
        return 0

    lax.fori_loop(0, ny, slopes, 0)

    def mirror_r(y):
        for m in range(1, mirrors):
            got_r(y, slab_of(m))
            rsend4(y, m).start()

    def smooth(y):
        for m in range(mirrors):
            got_r(y, m * 2 + 1 - core)
        r = unpack(R[y], dz, nx)
        zh, zl = zs[0], zs[1]
        xh, xl = xs[0], xs[1]
        for c in range(3):
            fh, fl = split(r * S[y, c])
            a = dot(zh, fh) + (dot(zh, fl) + dot(zl, fh))
            ah, al = split(a)
            o_v[c, :, y, :] = dot(ah, xh) + (dot(ah, xl) + dot(al, xh))

    mirror_r(0)

    def steps(y, _):
        @pl.when(y + 1 < ny)
        def _():
            mirror_r(y + 1)
        smooth(y)
        return 0

    lax.fori_loop(0, ny, steps, 0)
    total = R[s, k]
    for i in range(1, n_subj):
        j = (s + i) % n_subj
        rdma(R.at[0, 0], acc.at[j], as_.at[0], a_recv.at[j], s, k).wait_recv()
        total = total + acc[j]
    nt_v[:, 0, :] = unpack(T[s + 1, k] + total / n_subj, dz, nx)

    for i in range(1, outer):
        send1(i).wait_send()
    for i in range(outer):
        y = i * 2 + par
        for m in range(mirrors):
            send2(y, m).wait_send()
        for m in range(1, mirrors):
            send3(y, m).wait_send()

    def drain(y, _):
        for m in range(1, mirrors):
            rsend3(y, m).wait_send()
        for m in range(mirrors):
            send4(y, m).wait_send()
            rsend4(y, m).wait_send()

        @pl.when(y != s)
        def _():
            asend(y).wait_send()

        @pl.when(k < n_slab - 1)
        def _():
            edge_up(y).wait_send()

        @pl.when(k > 0)
        def _():
            edge_down(y).wait_send()
        return 0

    lax.fori_loop(0, ny, drain, 0)

def write_out(a, b, out, new_t, sems):
    copies = [pltpu.make_async_copy(a, out, sems.at[0]), pltpu.make_async_copy(b, new_t, sems.at[1])]
    for c in copies:
        c.start()
    for c in copies:
        c.wait()


def per_device(image, velocity, template, z_kernel, x_kernel):
    n_subj, n_slab = lax.axis_size("subj"), lax.axis_size("slab")
    _, dz, ny, nx = image.shape
    nz = n_slab * dz
    mirrors, outer = n_slab // 2, n_subj // 2
    f32, bf16 = jnp.float32, jnp.bfloat16
    dma = pltpu.SemaphoreType.DMA
    any_ = pl.BlockSpec(memory_space=pltpu.HBM)
    vmem = pl.BlockSpec(memory_space=pltpu.VMEM)
    pr = dz + dz * (nx % 128) // 128
    whole = (3, dz, ny, nx)
    a, b = pl.pallas_call(
        functools.partial(kernel, n_subj, n_slab, dz, nx),
        out_shape=(pltpu.VMEM(whole, f32), pltpu.VMEM(template.shape, f32)),
        in_specs=[any_] * 5,
        out_specs=(vmem, vmem),
        scratch_shapes=[
            pltpu.VMEM((ny, dz, nx), f32),
            pltpu.VMEM((3, ny, dz, nx), f32),
            pltpu.VMEM((dz, 1, nx), f32),
            pltpu.VMEM((nz, nz), f32),
            pltpu.VMEM((nx, nx), f32),
            pltpu.VMEM((ny + 2, n_slab, pr, 128), f32),
            pltpu.VMEM((ny, n_slab, pr, 128), f32),
            pltpu.VMEM((ny, 3, nz, nx), f32),
            pltpu.VMEM((2, ny, 1, nx), f32),
            pltpu.VMEM((ny, pr, 128), f32),
            pltpu.VMEM((2, dz, nz), bf16),
            pltpu.VMEM((2, nx, nx), bf16),
            dma((3,)),
            dma((4, ny)),
            dma((ny, n_slab)),
            dma((ny, n_slab)),
            dma((2, ny)),
            dma((ny,)),
            dma((outer,)),
            dma((outer, mirrors)),
            dma((outer, mirrors)),
            dma((ny, mirrors)),
            dma((ny, mirrors)),
            dma((ny, mirrors)),
            dma((2, ny)),
            dma((ny,)),
        ],
        compiler_params=pltpu.CompilerParams(
            collective_id=0, has_side_effects=True, vmem_limit_bytes=56 * 1024 * 1024
        ),
    )(image[0], velocity[0], template, z_kernel, x_kernel)
    update, new_template = pl.pallas_call(
        write_out,
        out_shape=(jax.ShapeDtypeStruct(whole, f32), jax.ShapeDtypeStruct(template.shape, f32)),
        in_specs=[vmem] * 2,
        out_specs=(any_, any_),
        scratch_shapes=[dma((2,))],
    )(a, b)
    return update[None], new_template


def solution(mesh):
    in_specs = (
        P("subj", "slab", None, None),
        P("subj", None, "slab", None, None),
        P("slab", "subj", None),
        P(),
        P(),
    )
    out_specs = (P("subj", None, "slab", None, None), P("slab", "subj", None))
    return jax.shard_map(
        per_device, mesh=mesh, in_specs=in_specs, out_specs=out_specs, check_vma=False
    )
```

time: 36.6 us -> 39.2 us (1.071)
  Pallas kernels: 32.8 us -> 36.7 us
  local copies, waits for them, and re-layouts: 3 us -> 1.62 us
    pallas_call x0 -> x1, Pallas kernels: none -> 2.3 us  [per_device(): pl.pallas_call(write_out, out_shape=(jax.ShapeDtypeStruct(whole, f32), ja...]
    pallas_call x1, Pallas kernels: 32.8 us -> 34.4 us  [per_device(): pl.pallas_call(functools.partial(kernel, n_subj, n_slab, dz, nx), out_sha...]
    unnamed x4, local copies, waits for them, and re-layouts: 3 us -> 1.62 us
where the time goes in v2:
time: 39.2 us; the launch traced here: 38.9 us
  Pallas kernels  36.7 us (94%)
  local copies, waits for them, and re-layouts  1.62 us (4%)
  between operations  0.65 us (2%)
    pallas_call x1, Pallas kernels, per_device(): pl.pallas_call(functools.partial(kernel, n_subj, n_slab, dz, nx), out_sha...  34.4 us
    pallas_call x1, Pallas kernels, per_device(): pl.pallas_call(write_out, out_shape=(jax.ShapeDtypeStruct(whole, f32), ja...  2.3 us
    unnamed x4, local copies, waits for them, and re-layouts  1.62 us

profile of v2, /device:TPU:0, one launch (start us, length us, event | category | flops | bytes accessed | tf_op | source)
XLA Modules:
  0.0 38.9 jit_solution(12508873218066599794)
XLA Ops:
  0.6 34.4 %shard_map.68 = (f32[3,48,8,192]{3,2,1,0:T(8,128)S(1)}, f32[48,1,192]{2,1,0:T(1,128)S(1)}) custom-call(f32[48,8,192]{2,1,0:T(8,128)} %bitcast.4, f32[3,48,8,192]{3,2,1,0:T(8,128)} %bitcast.3, f32[48,1,192]{2,1,0:T(1,128)} %template.1, f32[192,192]{1,0:T(8,128)} %zk.1, f32[192,192]{1,0:T(8,128)} %xk.1), custom_call_target="tpu_custom_call" | custom-call | tf_op jit(solution)/shard_map/pallas_call | solution.py:366
  35.0 0.0 copy-start
  35.0 1.0 %copy-done = f32[3,48,8,192]{3,2,1,0:T(8,128)} copy-done((f32[3,48,8,192]{3,2,1,0:T(8,128)}, f32[3,48,8,192]{3,2,1,0:T(8,128)S(1)}, u32[]{:S(2)}) %copy-start) | copy-done | bytes 884760
  36.0 0.0 copy-start.1
  36.0 0.6 %copy-done.1 = f32[48,1,192]{2,1,0:T(1,128)} copy-done((f32[48,1,192]{2,1,0:T(1,128)}, f32[48,1,192]{2,1,0:T(1,128)S(1)}, u32[]{:S(2)}) %copy-start.1) | copy-done | bytes 36888
  36.6 2.3 %shard_map.69 = (f32[3,48,8,192]{3,2,1,0:T(8,128)}, f32[48,1,192]{2,1,0:T(1,128)}) custom-call(f32[3,48,8,192]{3,2,1,0:T(8,128)} %copy-done, f32[48,1,192]{2,1,0:T(1,128)} %copy-done.1), custom_call_target="tpu_custom_call" | custom-call | tf_op jit(solution)/shard_map/pallas_call | solution.py:403
Async XLA Ops:
  35.0 1.0 %copy-start = (f32[3,48,8,192]{3,2,1,0:T(8,128)}, f32[3,48,8,192]{3,2,1,0:T(8,128)S(1)}, u32[]{:S(2)}) copy-start(f32[3,48,8,192]{3,2,1,0:T(8,128)S(1)} %get-tuple-element.6.a) | copy-start | bytes 2654212
  36.0 0.6 %copy-start.1 = (f32[48,1,192]{2,1,0:T(1,128)}, f32[48,1,192]{2,1,0:T(1,128)S(1)}, u32[]{:S(2)}) copy-start(f32[48,1,192]{2,1,0:T(1,128)S(1)} %get-tuple-element.7.b) | copy-start | bytes 110596

commit v3 on v2

--- a/solution.py
+++ b/solution.py
@@ -54,9 +54,9 @@
 
 def kernel(
     n_subj, n_slab, dz, nx,
-    image, velocity, template, zk, xk, o_v, nt_v,
-    img_v, vel_v, row_v, zk_v, xk_v, T, R, S, E, acc, zs, xs,
-    loc, in_sem, t_recv, r_recv, e_recv, a_recv,
+    image, velocity, template, zk, z_out, nt_out,
+    raw_v, field_v, row_v, zk_v, T, R, S, E, acc, zs, zh, z_v, nt_v,
+    loc, in_sem, z_sem, t_recv, r_recv, e_recv, a_recv,
     s1, s2, s3, s4, r3, r4, es, as_,
 ):
     ny = n_subj
@@ -73,21 +73,17 @@
     cps = [
         pltpu.make_async_copy(template, row_v, loc.at[0]),
         pltpu.make_async_copy(zk, zk_v, loc.at[1]),
-        pltpu.make_async_copy(xk, xk_v, loc.at[2]),
+    ] + [
+        pltpu.make_async_copy(velocity.at[c], raw_v.at[c], in_sem.at[c]) for c in range(3)
+    ] + [
+        pltpu.make_async_copy(image, raw_v.at[3], in_sem.at[3])
     ]
     for c in cps:
         c.start()
 
-    def row_in(y):
-        return [pltpu.make_async_copy(image.at[:, y, :], img_v.at[y], in_sem.at[3, y])] + [
-            pltpu.make_async_copy(velocity.at[c, :, y, :], vel_v.at[c, y], in_sem.at[c, y])
-            for c in range(3)
-        ]
-
-    def load_rows(y, _):
-        for c in row_in(y):
-            c.start()
-        return 0
+    def transpose(c):
+        cps[2 + c].wait()
+        field_v[c] = jnp.swapaxes(raw_v[c], 0, 1)
 
     E[...] = jnp.zeros_like(E)
     T[0] = jnp.zeros_like(T[0])
@@ -188,8 +184,9 @@
 
     for m in range(1, mirrors):
         send3(s, m).start()
-    lax.fori_loop(0, ny, load_rows, 0)
     send4(s, 0).start()
+    transpose(0)
+    transpose(1)
     for i in range(1, outer):
         y = ((so + i) % outer) * 2 + par
         got_t(y, k)
@@ -197,6 +194,12 @@
         for m in range(1, mirrors):
             send3(y, m).start()
         send4(y, 0).start()
+        if i == 1:
+            transpose(2)
+        if i == 2:
+            transpose(3)
+    if outer < 3:
+        transpose(3)
     for i in range(outer):
         y = ((so + i) % outer) * 2 + 1 - par
         got_t(y, k)
@@ -221,10 +224,8 @@
         sz = z_slope(t, E[0, y], E[1, y])
         sy = unpack((T[y + 2, k] - T[y, k]) * 0.5, dz, nx)
         sx = x_slope(t)
-        for c in row_in(y):
-            c.wait()
-        v = [vel_v[c, y] for c in range(3)]
-        R[y, k] = pack(img_v[y] - (t + (v[0] * sz + v[1] * sy + v[2] * sx)))
+        v = [field_v[c, y] for c in range(3)]
+        R[y, k] = pack(field_v[3, y] - (t + (v[0] * sz + v[1] * sy + v[2] * sx)))
         for m in range(1, mirrors):
             rsend3(y, m).start()
         rsend4(y, 0).start()
@@ -245,16 +246,13 @@
     lax.fori_loop(0, ny, residual, 0)
 
     cps[1].wait()
-    cps[2].wait()
     for j in range(n_slab):
         @pl.when(j == k)
         def _():
-            hi, lo = split(zk_v[j * dz:(j + 1) * dz, :])
-            zs[0] = hi
-            zs[1] = lo
-    hi, lo = split(xk_v[...].T)
-    xs[0] = hi
-    xs[1] = lo
+            rows = zk_v[j * dz:(j + 1) * dz, :]
+            hi = rows.astype(jnp.bfloat16).astype(jnp.float32)
+            zs[...] = jnp.concatenate([hi, rows - hi], axis=0).astype(jnp.bfloat16)
+            zh[...] = hi.astype(jnp.bfloat16)
 
     for i in range(outer):
         y = ((so + i) % outer) * 2 + 1 - par
@@ -285,33 +283,42 @@
             rsend4(y, m).start()
 
     def smooth(y):
-        for m in range(mirrors):
-            got_r(y, m * 2 + 1 - core)
         r = unpack(R[y], dz, nx)
-        zh, zl = zs[0], zs[1]
-        xh, xl = xs[0], xs[1]
         for c in range(3):
             fh, fl = split(r * S[y, c])
-            a = dot(zh, fh) + (dot(zh, fl) + dot(zl, fh))
-            ah, al = split(a)
-            o_v[c, :, y, :] = dot(ah, xh) + (dot(ah, xl) + dot(al, xh))
+            p = dot(zs[...], fh)
+            z_v[c, y] = p[:dz] + (p[dz:] + dot(zh[...], fl))
+
+    def z_copy(g):
+        part = pl.ds(g * 2, 2)
+        return pltpu.make_async_copy(z_v.at[:, part], z_out.at[:, part], z_sem.at[g])
 
     mirror_r(0)
-
-    def steps(y, _):
-        @pl.when(y + 1 < ny)
-        def _():
-            mirror_r(y + 1)
-        smooth(y)
+    mirror_r(1)
+
+    def steps(g, _):
+        @pl.when(g + 1 < ny // 2)
+        def _():
+            mirror_r(2 * g + 2)
+            mirror_r(2 * g + 3)
+        for i in range(2):
+            for m in range(mirrors):
+                got_r(2 * g + i, m * 2 + 1 - core)
+        for i in range(2):
+            smooth(2 * g + i)
+        z_copy(g).start()
         return 0
 
-    lax.fori_loop(0, ny, steps, 0)
+    lax.fori_loop(0, ny // 2, steps, 0)
+
     total = R[s, k]
     for i in range(1, n_subj):
         j = (s + i) % n_subj
         rdma(R.at[0, 0], acc.at[j], as_.at[0], a_recv.at[j], s, k).wait_recv()
         total = total + acc[j]
     nt_v[:, 0, :] = unpack(T[s + 1, k] + total / n_subj, dz, nx)
+    n_cp = pltpu.make_async_copy(nt_v, nt_out, loc.at[2])
+    n_cp.start()
 
     for i in range(1, outer):
         send1(i).wait_send()
@@ -343,13 +350,32 @@
         return 0
 
     lax.fori_loop(0, ny, drain, 0)
-
-def write_out(a, b, out, new_t, sems):
-    copies = [pltpu.make_async_copy(a, out, sems.at[0]), pltpu.make_async_copy(b, new_t, sems.at[1])]
-    for c in copies:
-        c.start()
-    for c in copies:
-        c.wait()
+    for g in range(ny // 2):
+        z_copy(g).wait()
+    n_cp.wait()
+
+
+def smooth_x(z_in, nt_in, xk, out, new_t, z_v, xk_v, o_v, in_sem, out_sem):
+    _, ny, dz, nx = z_in.shape
+    nt_copy = pltpu.make_async_copy(nt_in, new_t, out_sem.at[3])
+    xk_copy = pltpu.make_async_copy(xk, xk_v, in_sem.at[3])
+    loads = [pltpu.make_async_copy(z_in.at[c], z_v.at[c], in_sem.at[c]) for c in range(3)]
+    stores = [pltpu.make_async_copy(o_v.at[c], out.at[c], out_sem.at[c]) for c in range(3)]
+    xk_copy.start()
+    for copy in loads:
+        copy.start()
+    nt_copy.start()
+    xk_copy.wait()
+    xh, xl = split(xk_v[...].T)
+    for c in range(3):
+        loads[c].wait()
+        ah, al = split(z_v[c].reshape(ny * dz, nx))
+        o = dot(ah, xh) + (dot(ah, xl) + dot(al, xh))
+        o_v[c] = jnp.swapaxes(o.reshape(ny, dz, nx), 0, 1)
+        stores[c].start()
+    for copy in stores:
+        copy.wait()
+    nt_copy.wait()
 
 
 def per_device(image, velocity, template, z_kernel, x_kernel):
@@ -360,29 +386,35 @@
     f32, bf16 = jnp.float32, jnp.bfloat16
     dma = pltpu.SemaphoreType.DMA
     any_ = pl.BlockSpec(memory_space=pltpu.HBM)
-    vmem = pl.BlockSpec(memory_space=pltpu.VMEM)
     pr = dz + dz * (nx % 128) // 128
+    by_row = (3, ny, dz, nx)
     whole = (3, dz, ny, nx)
-    a, b = pl.pallas_call(
+    grant = 56 * 1024 * 1024
+    smoothed, updated = pl.pallas_call(
         functools.partial(kernel, n_subj, n_slab, dz, nx),
-        out_shape=(pltpu.VMEM(whole, f32), pltpu.VMEM(template.shape, f32)),
-        in_specs=[any_] * 5,
-        out_specs=(vmem, vmem),
+        out_shape=(
+            jax.ShapeDtypeStruct(by_row, f32),
+            jax.ShapeDtypeStruct(template.shape, f32),
+        ),
+        in_specs=[any_] * 4,
+        out_specs=(any_, any_),
         scratch_shapes=[
-            pltpu.VMEM((ny, dz, nx), f32),
-            pltpu.VMEM((3, ny, dz, nx), f32),
+            pltpu.VMEM((4, dz, ny, nx), f32),
+            pltpu.VMEM((4, ny, dz, nx), f32),
             pltpu.VMEM((dz, 1, nx), f32),
             pltpu.VMEM((nz, nz), f32),
-            pltpu.VMEM((nx, nx), f32),
             pltpu.VMEM((ny + 2, n_slab, pr, 128), f32),
             pltpu.VMEM((ny, n_slab, pr, 128), f32),
             pltpu.VMEM((ny, 3, nz, nx), f32),
             pltpu.VMEM((2, ny, 1, nx), f32),
             pltpu.VMEM((ny, pr, 128), f32),
-            pltpu.VMEM((2, dz, nz), bf16),
-            pltpu.VMEM((2, nx, nx), bf16),
+            pltpu.VMEM((2 * dz, nz), bf16),
+            pltpu.VMEM((dz, nz), bf16),
+            pltpu.VMEM(by_row, f32),
+            pltpu.VMEM((dz, 1, nx), f32),
             dma((3,)),
-            dma((4, ny)),
+            dma((4,)),
+            dma((ny // 2,)),
             dma((ny, n_slab)),
             dma((ny, n_slab)),
             dma((2, ny)),
@@ -397,16 +429,23 @@
             dma((ny,)),
         ],
         compiler_params=pltpu.CompilerParams(
-            collective_id=0, has_side_effects=True, vmem_limit_bytes=56 * 1024 * 1024
+            collective_id=0, has_side_effects=True, vmem_limit_bytes=grant
         ),
-    )(image[0], velocity[0], template, z_kernel, x_kernel)
+    )(image[0], velocity[0], template, z_kernel)
     update, new_template = pl.pallas_call(
-        write_out,
+        smooth_x,
         out_shape=(jax.ShapeDtypeStruct(whole, f32), jax.ShapeDtypeStruct(template.shape, f32)),
-        in_specs=[vmem] * 2,
+        in_specs=[any_] * 3,
         out_specs=(any_, any_),
-        scratch_shapes=[dma((2,))],
-    )(a, b)
+        scratch_shapes=[
+            pltpu.VMEM(by_row, f32),
+            pltpu.VMEM((nx, nx), f32),
+            pltpu.VMEM(whole, f32),
+            dma((4,)),
+            dma((4,)),
+        ],
+        compiler_params=pltpu.CompilerParams(vmem_limit_bytes=grant),
+    )(smoothed, updated, x_kernel)
     return update[None], new_template
 
 

time: 39.2 us -> 35.1 us (0.90)
  Pallas kernels: 36.7 us -> 33.9 us
  local copies, waits for them, and re-layouts: 1.62 us -> 0 us
    pallas_call x1, Pallas kernels: 34.4 us -> 30.7 us  [per_device(): pl.pallas_call(functools.partial(kernel, n_subj, n_slab, dz, nx), out_sha...]
    unnamed x4 -> x0, local copies, waits for them, and re-layouts: 1.62 us -> none
    pallas_call x1, Pallas kernels: 2.3 us -> 3.24 us  [per_device(): pl.pallas_call(smooth_x, out_shape=(jax.ShapeDtypeStruct(whole, f32), jax...]
where the time goes in v3:
time: 35.1 us; the launch traced here: 34.6 us
  Pallas kernels  33.9 us (97%)
  between operations  0.64 us (2%)
    pallas_call x1, Pallas kernels, per_device(): pl.pallas_call(functools.partial(kernel, n_subj, n_slab, dz, nx), out_sha...  30.7 us
    pallas_call x1, Pallas kernels, per_device(): pl.pallas_call(smooth_x, out_shape=(jax.ShapeDtypeStruct(whole, f32), jax...  3.24 us

profile of v3, /device:TPU:0, one launch (start us, length us, event | category | flops | bytes accessed | tf_op | source)
XLA Modules:
  0.0 34.6 jit_solution(14339098922635046757)
XLA Ops:
  0.6 30.7 %shard_map.68 = (f32[3,8,48,192]{3,2,1,0:T(8,128)}, f32[48,1,192]{2,1,0:T(1,128)}) custom-call(f32[48,8,192]{2,1,0:T(8,128)} %bitcast.4, f32[3,48,8,192]{3,2,1,0:T(8,128)} %bitcast.3, f32[48,1,192]{2,1,0:T(1,128)} %template.1, f32[192,192]{1,0:T(8,128)} %zk.1), custom_call_target="tpu_custom_call" | custom-call | tf_op jit(solution)/shard_map/pallas_call | solution.py:393
  31.3 3.2 %shard_map.69 = (f32[3,48,8,192]{3,2,1,0:T(8,128)}, f32[48,1,192]{2,1,0:T(1,128)}) custom-call(f32[3,8,48,192]{3,2,1,0:T(8,128)} %get-tuple-element.6.z_in, f32[48,1,192]{2,1,0:T(1,128)} %get-tuple-element.7.nt_in, f32[192,192]{1,0:T(8,128)} %xk.1), custom_call_target="tpu_custom_call" | custom-call | tf_op jit(solution)/shard_map/pallas_call | solution.py:435

commit v4 on v3

--- a/solution.py
+++ b/solution.py
@@ -265,22 +265,26 @@
             got_t(y, m * 2 + 1 - core)
         return 0
 
-    lax.fori_loop(0, ny, sibling_t, 0)
+    sibling_t(0, 0)
+
+    def mirror_r(y):
+        for m in range(1, mirrors):
+            got_r(y, slab_of(m))
+            rsend4(y, m).start()
 
     def slopes(y, _):
+        @pl.when(y + 1 < ny)
+        def _():
+            sibling_t(y + 1, 0)
         zero = jnp.zeros((1, nx), jnp.float32)
         t = unpack(T[y + 1], dz, nx)
         S[y, 0] = z_slope(t, zero, zero)
         S[y, 1] = unpack((T[y + 2] - T[y]) * 0.5, dz, nx)
         S[y, 2] = x_slope(t)
+        mirror_r(y)
         return 0
 
     lax.fori_loop(0, ny, slopes, 0)
-
-    def mirror_r(y):
-        for m in range(1, mirrors):
-            got_r(y, slab_of(m))
-            rsend4(y, m).start()
 
     def smooth(y):
         r = unpack(R[y], dz, nx)
@@ -293,14 +297,7 @@
         part = pl.ds(g * 2, 2)
         return pltpu.make_async_copy(z_v.at[:, part], z_out.at[:, part], z_sem.at[g])
 
-    mirror_r(0)
-    mirror_r(1)
-
     def steps(g, _):
-        @pl.when(g + 1 < ny // 2)
-        def _():
-            mirror_r(2 * g + 2)
-            mirror_r(2 * g + 3)
         for i in range(2):
             for m in range(mirrors):
                 got_r(2 * g + i, m * 2 + 1 - core)

time: 35.1 us -> 33.1 us (0.943)
  Pallas kernels: 33.9 us -> 32.1 us
    pallas_call x1, Pallas kernels: 30.7 us -> 28.8 us  [per_device(): pl.pallas_call(functools.partial(kernel, n_subj, n_slab, dz, nx), out_sha...]
where the time goes in v4:
time: 33.1 us; the launch traced here: 32.7 us
  Pallas kernels  32.1 us (97%)
  between operations  0.64 us (2%)
    pallas_call x1, Pallas kernels, per_device(): pl.pallas_call(functools.partial(kernel, n_subj, n_slab, dz, nx), out_sha...  28.8 us
    pallas_call x1, Pallas kernels, per_device(): pl.pallas_call(smooth_x, out_shape=(jax.ShapeDtypeStruct(whole, f32), jax...  3.24 us

profile of v4, /device:TPU:0, one launch (start us, length us, event | category | flops | bytes accessed | tf_op | source)
XLA Modules:
  0.0 32.7 jit_solution(2967761682839975497)
XLA Ops:
  0.6 28.8 %shard_map.68 = (f32[3,8,48,192]{3,2,1,0:T(8,128)}, f32[48,1,192]{2,1,0:T(1,128)}) custom-call(f32[48,8,192]{2,1,0:T(8,128)} %bitcast.4, f32[3,48,8,192]{3,2,1,0:T(8,128)} %bitcast.3, f32[48,1,192]{2,1,0:T(1,128)} %template.1, f32[192,192]{1,0:T(8,128)} %zk.1), custom_call_target="tpu_custom_call" | custom-call | tf_op jit(solution)/shard_map/pallas_call | solution.py:390
  29.5 3.2 %shard_map.69 = (f32[3,48,8,192]{3,2,1,0:T(8,128)}, f32[48,1,192]{2,1,0:T(1,128)}) custom-call(f32[3,8,48,192]{3,2,1,0:T(8,128)} %get-tuple-element.6.z_in, f32[48,1,192]{2,1,0:T(1,128)} %get-tuple-element.7.nt_in, f32[192,192]{1,0:T(8,128)} %xk.1), custom_call_target="tpu_custom_call" | custom-call | tf_op jit(solution)/shard_map/pallas_call | solution.py:432
